TPU v7x, 32 devices: a whole 2x2x4 slice. The times are simulated.
32 devices in a mesh: grp: 2 (over y), row: 4 (over z), col: 4 (over x, core).
Axes of the slice: x: 2, y: 2, z: 4, core: 2. Of those that a mesh axis runs over, the one named last changes fastest.
Arguments:
- pair: bfloat16 [128, 64, 128], P(('grp', 'row'), 'col'), parts along dimension 0, may hold values from -6 to 6
- cotangent: bfloat16 [128, 64, 128], P(('grp', 'row'), 'col'), parts along dimension 0, may hold values from -6 to 6
- lengths: int32 [2], P('grp'), parts along dimension 0, may hold values from 32 to 64
- norm_in_gain: float32 [128], replicated, may hold values from 0.25 to 1.75
- norm_in_bias: float32 [128], replicated, may hold values from -3 to 3
- left_weight: bfloat16 [128, 256], replicated, may hold values from -0.5 to 0.5
- right_weight: bfloat16 [128, 256], replicated, may hold values from -0.5 to 0.5
- gate_weight: bfloat16 [128, 128], replicated, may hold values from -0.5 to 0.5
- norm_mid_gain: float32 [128], replicated, may hold values from 0.25 to 1.75
- norm_mid_bias: float32 [128], replicated, may hold values from -3 to 3
- out_weight: bfloat16 [128, 128], replicated, may hold values from -0.5 to 0.5
Outputs:
- result: bfloat16 [128, 64, 128], P(('grp', 'row'), 'col'), parts along dimension 0
- grad_pair: float32 [128, 64, 128], P(('grp', 'row'), 'col'), parts along dimension 0
- d_left: float32 [256, 256], P('grp'), parts along dimension 0
- d_right: float32 [256, 256], P('grp'), parts along dimension 0
- d_gate: float32 [256, 128], P('grp'), parts along dimension 0
- d_out: float32 [256, 128], P('grp'), parts along dimension 0
- d_norm_in: float32 [4, 128], P('grp'), parts along dimension 0
- d_norm_mid: float32 [4, 128], P('grp'), parts along dimension 0
There are 2 independent parts, one for each index of `grp`. A program takes and returns all parts, laid end to end along the dimension named above; an argument that names none is the same for every part. Nothing has to cross between parts.
All inputs are finite; a program needn't handle non-finite values.
Results may differ from a plain program's by a relative error of at most 0.0072.
Values may be sent and summed in bfloat16 or wider, within the bound.
A program may use at most 64 MiB of HBM per device.

v0:
```python
import jax
import jax.numpy as jnp
from jax import lax
from jax.sharding import PartitionSpec as P

EPS = 1e-05


def from_root(x, axis, root):
    mine = lax.axis_index(axis) == root
    return lax.psum(jnp.where(mine, x, jnp.zeros_like(x)), axis)


def normalize(value, gain, bias):
    centre = value - jnp.mean(value, axis=-1, keepdims=True)
    spread = lax.rsqrt(jnp.mean(centre * centre, axis=-1, keepdims=True) + EPS)
    scaled = centre * spread
    return (scaled * gain + bias, scaled, spread)


def norm_back(upstream, gain, scaled, spread):
    inner_grad = upstream * gain
    centred = inner_grad - jnp.mean(inner_grad, axis=-1, keepdims=True)
    return spread * (centred - scaled * jnp.mean(inner_grad * scaled, axis=-1, keepdims=True))


def gated_half(normed, weight, pair_mask):
    projected = jnp.dot(normed, weight, preferred_element_type=jnp.float32)
    half_width = weight.shape[1] // 2
    values = projected[..., :half_width]
    switch = jax.nn.sigmoid(projected[..., half_width:])
    return (pair_mask * switch * values, values, switch)


def gated_back(upstream, pair_mask, values, switch):
    first = upstream * pair_mask * switch
    second = upstream * pair_mask * values * switch * (1.0 - switch)
    return jnp.concatenate([first, second], axis=-1).astype(jnp.bfloat16)


def flip_pair(block, block_rows):
    lined = lax.all_gather(block, "col", axis=1, tiled=True)
    fetched = from_root(lined, "row", lax.axis_index("col"))
    return lax.dynamic_slice_in_dim(fetched, lax.axis_index("row") * block_rows, block_rows, 1)


def flip_grad(block, block_rows):
    lined = lax.all_gather(block.astype(jnp.bfloat16), "col", axis=1, tiled=True).astype(
        block.dtype
    )
    fetched = from_root(lined.astype(jnp.bfloat16), "row", lax.axis_index("col")).astype(
        lined.dtype
    )
    return lax.dynamic_slice_in_dim(fetched, lax.axis_index("row") * block_rows, block_rows, 1)


def cell_sum(first, second):
    return jnp.einsum("ijc,ijh->ch", first, second, preferred_element_type=jnp.float32)


def on_device(
    pair,
    cotangent,
    lengths,
    norm_in_gain,
    norm_in_bias,
    left_weight,
    right_weight,
    gate_weight,
    norm_mid_gain,
    norm_mid_bias,
    out_weight,
):
    block_rows = pair.shape[0]
    row_place = lax.axis_index("row")
    col_place = lax.axis_index("col")
    offsets = jnp.arange(block_rows, dtype=jnp.int32)

    def valid_from(place):
        return (place * block_rows + offsets < lengths[0]).astype(jnp.float32)

    mask_near = valid_from(row_place)[:, None, None] * valid_from(col_place)[None, :, None]
    mask_far = valid_from(col_place)[:, None, None] * valid_from(row_place)[None, :, None]
    flipped = flip_pair(pair, block_rows)
    normed, scaled_in, spread_in = normalize(pair.astype(jnp.float32), norm_in_gain, norm_in_bias)
    normed_b = normed.astype(jnp.bfloat16)
    normed_far = normalize(flipped.astype(jnp.float32), norm_in_gain, norm_in_bias)[0].astype(
        jnp.bfloat16
    )
    left, left_values, left_switch = gated_half(normed_b, left_weight, mask_near)
    right, right_values, right_switch = gated_half(normed_far, right_weight, mask_far)
    left_rows = lax.all_gather(left.astype(jnp.bfloat16), "col", axis=1, tiled=True)
    right_rows = lax.all_gather(right.astype(jnp.bfloat16), "row", axis=1, tiled=True)
    product = jnp.einsum("ikh,jkh->ijh", left_rows, right_rows, preferred_element_type=jnp.float32)
    mixed, scaled_mid, spread_mid = normalize(product, norm_mid_gain, norm_mid_bias)
    mixed_b = mixed.astype(jnp.bfloat16)
    update = jnp.dot(mixed_b, out_weight, preferred_element_type=jnp.float32)
    switch_out = jax.nn.sigmoid(jnp.dot(normed_b, gate_weight, preferred_element_type=jnp.float32))
    result = (switch_out * update).astype(jnp.bfloat16)
    upstream = cotangent.astype(jnp.float32)
    grad_update = (upstream * switch_out).astype(jnp.bfloat16)
    grad_gate = (upstream * update * switch_out * (1.0 - switch_out)).astype(jnp.bfloat16)
    grad_mixed = jnp.dot(grad_update, out_weight.T, preferred_element_type=jnp.float32)
    grad_product = norm_back(grad_mixed, norm_mid_gain, scaled_mid, spread_mid).astype(jnp.bfloat16)
    piece = right_rows
    grad_left = jnp.transpose(
        lax.psum_scatter(
            jnp.einsum("ijh,jkh->kih", grad_product, piece, preferred_element_type=jnp.float32),
            "col",
            scatter_dimension=0,
            tiled=True,
        ),
        (1, 0, 2),
    )
    piece = left_rows
    grad_right = jnp.transpose(
        lax.psum_scatter(
            jnp.einsum("ijh,ikh->kjh", grad_product, piece, preferred_element_type=jnp.float32),
            "row",
            scatter_dimension=0,
            tiled=True,
        ),
        (1, 0, 2),
    )
    left_back = gated_back(grad_left, mask_near, left_values, left_switch)
    right_back = gated_back(grad_right, mask_far, right_values, right_switch)
    far_grad = jnp.dot(right_back, right_weight.T, preferred_element_type=jnp.float32)
    grad_normed = jnp.dot(left_back, left_weight.T, preferred_element_type=jnp.float32)
    grad_normed = grad_normed + jnp.dot(
        grad_gate, gate_weight.T, preferred_element_type=jnp.float32
    )
    grad_normed = grad_normed + flip_grad(far_grad, block_rows)
    grad_pair = norm_back(grad_normed, norm_in_gain, scaled_in, spread_in)
    sum_left = cell_sum(normed_b, left_back)
    sum_right = cell_sum(normed_far, right_back)
    sum_gate = cell_sum(normed_b, grad_gate)
    sum_out = cell_sum(mixed_b, grad_update)
    sum_norm_in = jnp.stack(
        [jnp.sum(grad_normed * scaled_in, axis=(0, 1)), jnp.sum(grad_normed, axis=(0, 1))]
    )
    sum_norm_mid = jnp.stack(
        [jnp.sum(grad_mixed * scaled_mid, axis=(0, 1)), jnp.sum(grad_mixed, axis=(0, 1))]
    )
    partial_sums = lax.psum(
        (sum_left, sum_right, sum_gate, sum_out, sum_norm_in, sum_norm_mid), "row"
    )
    totals = lax.psum(
        (
            partial_sums[0],
            partial_sums[1],
            partial_sums[2],
            partial_sums[3],
            partial_sums[4],
            partial_sums[5],
        ),
        "col",
    )
    factor = 1.0 / (block_rows * lax.axis_size("row"))
    return (
        result,
        grad_pair,
        totals[0] * factor,
        totals[1] * factor,
        totals[2] * factor,
        totals[3] * factor,
        totals[4] * factor,
        totals[5] * factor,
    )


def solution(mesh):
    in_specs = (
        P(("grp", "row"), "col", None),
        P(("grp", "row"), "col", None),
        P("grp"),
        P(),
        P(),
        P(),
        P(),
        P(),
        P(),
        P(),
        P(),
    )
    out_specs = (
        P(("grp", "row"), "col", None),
        P(("grp", "row"), "col", None),
        P("grp", None),
        P("grp", None),
        P("grp", None),
        P("grp", None),
        P("grp", None),
        P("grp", None),
    )
    return jax.shard_map(
        on_device, mesh=mesh, in_specs=in_specs, out_specs=out_specs, check_vma=False
    )
```

profile of v0, /device:TPU:0, one launch (start us, length us, event | category | flops | bytes accessed | tf_op | source)
XLA Modules:
  0.0 244.5 jit_solution(9429052326201666448)
XLA Ops:
  7.2 7.4 %all_gather.12 = bf16[16,64,128]{2,1,0:T(8,128)(2,1)S(1)} all-gather(bf16[16,16,128]{2,1,0:T(8,128)(2,1)} %param.11), channel_id=1, replica_groups=mesh['grp'=2,'row'=4,'col'=4] {'col'}, dimensions={1}, use_global_device_ids=true | all-gather | bytes 327680 | tf_op jit(solution)/shard_map/all_gather | solution.py:42
  14.6 0.7 broadcast_select_fusion.1
  15.4 0.8 copy-done.1
  18.6 5.9 %all_gather.14 = bf16[16,64,128]{2,1,0:T(8,128)(2,1)S(1)} all-gather(bf16[16,16,128]{2,1,0:T(8,128)(2,1)S(1)} %multiply_convert_fusion.6), channel_id=1, replica_groups=mesh['grp'=2,'row'=4,'col'=4] {'col'}, dimensions={1}, use_global_device_ids=true | all-gather | bytes 327680 | tf_op jit(solution)/shard_map/all_gather | solution.py:92
  24.9 27.3 %all-reduce.9.cloned.1.call-done = bf16[16,64,128]{2,1,0:T(8,128)(2,1)} async-done(((bf16[16,64,128]{2,1,0:T(8,128)(2,1)}), bf16[16,64,128]{2,1,0:T(8,128)(2,1)}) %all-reduce.9.cloned.1.call-update) | async-done | bytes 262160 | tf_op jit(solution)/shard_map/psum | solution.py:11
  52.2 0.9 convert_reduce_fusion
  53.1 1.0 fusion.12
  54.2 1.1 fusion.38
  55.5 14.4 %all_gather.13 = bf16[16,64,128]{2,1,0:T(8,128)(2,1)S(1)} all-gather(bf16[16,16,128]{2,1,0:T(8,128)(2,1)S(1)} %multiply_convert_fusion.7), channel_id=1, replica_groups=mesh['grp'=2,'row'=4,'col'=4] {'row'}, dimensions={1}, use_global_device_ids=true | all-gather | bytes 327680 | tf_op jit(solution)/shard_map/all_gather | solution.py:93
  73.0 0.9 fusion.26
  73.9 0.7 multiply_reduce_fusion
  75.7 1.2 copy.86
  77.4 1.2 copy.83
  79.3 0.9 convolution_bitcast_fusion.3
  80.2 1.0 convolution_bitcast_fusion.2
  82.1 16.5 %reduce-scatter.5.cloned.1.call-done = f32[16,16,128]{2,0,1:T(8,128)} async-done(((f32[64,16,128]{2,0,1:T(8,128)}), f32[16,16,128]{2,0,1:T(8,128)}) %reduce-scatter.5.cloned.1.call-update) | async-done | bytes 131088 | tf_op jit(solution)/shard_map/reduce_scatter | solution.py:117
  98.6 1.0 multiply_convert_fusion.1
  99.8 5.8 %all_gather.15 = bf16[16,64,128]{2,1,0:T(8,128)(2,1)S(1)} all-gather(bf16[16,16,128]{2,1,0:T(8,128)(2,1)S(1)} %convolution_convert_fusion), channel_id=1, replica_groups=mesh['grp'=2,'row'=4,'col'=4] {'col'}, dimensions={1}, use_global_device_ids=true | all-gather | bytes 327680 | tf_op jit(solution)/shard_map/all_gather | solution.py:48
  105.6 0.7 broadcast_select_fusion
  106.4 14.8 %reduce-scatter.3.cloned.1.call-done = f32[16,16,128]{2,0,1:T(8,128)} async-done(((f32[64,16,128]{2,0,1:T(8,128)}), f32[16,16,128]{2,0,1:T(8,128)}) %reduce-scatter.3.cloned.1.call-update) | async-done | bytes 131088 | tf_op jit(solution)/shard_map/reduce_scatter | solution.py:107
  121.2 1.0 multiply_convert_fusion.3
  122.2 1.8 convolution_bitcast_fusion
  124.0 1.0 convolution_bitcast_fusion.1
  125.1 33.6 %all-reduce.11.cloned.1.call-done = bf16[16,64,128]{2,1,0:T(8,128)(2,1)} async-done(((bf16[16,64,128]{2,1,0:T(8,128)(2,1)}), bf16[16,64,128]{2,1,0:T(8,128)(2,1)}) %all-reduce.11.cloned.1.call-update) | async-done | bytes 262160 | tf_op jit(solution)/shard_map/psum | solution.py:11
  158.7 1.1 fusion.21
  159.9 10.8 %all-reduce.2 = (f32[2,128]{1,0:T(2,128)S(1)}, f32[2,128]{1,0:T(2,128)S(1)}) all-reduce(f32[2,128]{1,0:T(2,128)S(1)} %pad_maximum_fusion.6, f32[2,128]{1,0:T(2,128)S(1)} %pad_maximum_fusion.7), channel_id=1, replica_groups=mesh['grp'=2,'row'=4,'col'=4] {'row'}, use_global_device_ids=true, to_apply=%region_24.25 | all-reduce | flops 512 | bytes 4096 | tf_op jit(solution)/shard_map/psum | solution.py:144
  170.7 6.0 %all-reduce = (f32[2,128]{1,0:T(2,128)S(1)}, f32[2,128]{1,0:T(2,128)S(1)}) all-reduce(f32[2,128]{1,0:T(2,128)S(1)} %get-tuple-element.22, f32[2,128]{1,0:T(2,128)S(1)} %get-tuple-element.23), channel_id=1, replica_groups=mesh['grp'=2,'row'=4,'col'=4] {'col'}, use_global_device_ids=true, to_apply=%region_25.26 | all-reduce | flops 512 | bytes 4096 | tf_op jit(solution)/shard_map/psum | solution.py:147
  177.3 0.9 fusion.20
  178.2 21.2 %all-reduce.15.cloned.1.call-done = (f32[128,256]{1,0:T(8,128)}, f32[128,256]{1,0:T(8,128)}, f32[128,128]{1,0:T(8,128)}, f32[128,128]{1,0:T(8,128)}) async-done(((f32[128,256]{1,0:T(8,128)}, f32[128,256]{1,0:T(8,128)}, f32[128,128]{1,0:T(8,128)}, f32[128,128]{1,0:T(8,128)}), (f32[128,256]{1,0:T(8,128)}, f32[128,256]{1,0:T(8,128)}, f32[128,128]{1,0:T(8,128)}, ...) | async-done | bytes 393232 | tf_op jit(solution)/shard_map/psum | solution.py:144
  199.9 34.2 %all-reduce.13.cloned.1.call-done = (f32[128,256]{1,0:T(8,128)}, f32[128,256]{1,0:T(8,128)}, f32[128,128]{1,0:T(8,128)}, f32[128,128]{1,0:T(8,128)}) async-done(((f32[128,256]{1,0:T(8,128)}, f32[128,256]{1,0:T(8,128)}, f32[128,128]{1,0:T(8,128)}, f32[128,128]{1,0:T(8,128)}), (f32[128,256]{1,0:T(8,128)}, f32[128,256]{1,0:T(8,128)}, f32[128,128]{1,0:T(8,128)}, ...) | async-done | bytes 393232 | tf_op jit(solution)/shard_map/psum | solution.py:147
  234.1 1.6 broadcast_multiply_fusion.1
  237.0 0.7 broadcast_multiply_fusion
  (117 shorter events, 11.1 us)
Async XLA Ops:
  7.2 10.1 %copy-start = (bf16[128,256]{1,0:T(8,128)(2,1)S(1)}, bf16[128,256]{1,0:T(8,128)(2,1)}, u32[]{:S(2)}) copy-start(bf16[128,256]{1,0:T(8,128)(2,1)} %param.16) | copy-start | bytes 196612
  7.2 45.0 %all-reduce.9.cloned.1.call-start = ((), (), s32[]{:S(2)}) async-start(), calls=%async_computation.2 | async-start | bytes 524288 | tf_op jit(solution)/shard_map/psum | solution.py:11
  15.3 0.8 copy-start.1
  15.4 83.2 %reduce-scatter.5.cloned.1.call-start = ((), (), s32[]{:S(2)}) async-start(), calls=%async_computation.4 | async-start | bytes 655360 | tf_op jit(solution)/shard_map/reduce_scatter | solution.py:117
  17.0 55.4 %copy-start.3 = (f32[16,16]{1,0:T(8,128)}, f32[16,16]{1,0:T(8,128)S(1)}, u32[]{:S(2)}) copy-start(f32[16,16]{1,0:T(8,128)S(1)} %broadcast_multiply_fusion.12) | copy-start | bytes 3076
  17.2 55.2 %copy-start.6 = (f32[16,16]{1,0:T(8,128)}, f32[16,16]{1,0:T(8,128)S(1)}, u32[]{:S(2)}) copy-start(f32[16,16]{1,0:T(8,128)S(1)} %add_rsqrt_fusion.2) | copy-start | bytes 3076
  17.9 37.5 %copy-start.12 = (f32[16,16]{1,0:T(8,128)}, f32[16,16]{1,0:T(8,128)S(1)}, u32[]{:S(2)}) copy-start(f32[16,16]{1,0:T(8,128)S(1)} %get-tuple-element.35) | copy-start | bytes 3076
  53.1 1.1 copy-start.16
  53.1 1.1 copy-start.10
  54.2 1.1 copy-start.23
  71.2 0.8 copy-start.2
  72.1 0.8 copy-start.14
  72.1 0.8 copy-start.21
  76.9 44.2 %reduce-scatter.3.cloned.1.call-start = ((), (), s32[]{:S(2)}) async-start(), calls=%async_computation.3 | async-start | bytes 655360 | tf_op jit(solution)/shard_map/reduce_scatter | solution.py:107
  77.3 1.2 copy-start.4
  77.3 1.2 copy-start.7
  77.4 1.2 copy-start.18
  79.2 1.0 copy-start.15
  79.2 1.0 copy-start.26
  79.2 1.0 copy-start.34
  81.2 0.8 copy-start.22
  81.2 77.5 %all-reduce.11.cloned.1.call-start = ((), (), s32[]{:S(2)}) async-start(), calls=%async_computation.5 | async-start | bytes 524288 | tf_op jit(solution)/shard_map/psum | solution.py:11
  81.9 16.7 %copy-start.13 = (f32[16,16]{1,0:T(8,128)S(1)}, f32[16,16]{1,0:T(8,128)}, u32[]{:S(2)}) copy-start(f32[16,16]{1,0:T(8,128)} %copy-done.12) | copy-start | bytes 3076
  82.1 17.5 %copy-start.17 = (bf16[128,256]{1,0:T(8,128)(2,1)S(1)}, bf16[128,256]{1,0:T(8,128)(2,1)}, u32[]{:S(2)}) copy-start(bf16[128,256]{1,0:T(8,128)(2,1)} %param.17) | copy-start | bytes 196612
  106.3 14.9 %copy-start.9 = (f32[16,16]{1,0:T(8,128)S(1)}, f32[16,16]{1,0:T(8,128)}, u32[]{:S(2)}) copy-start(f32[16,16]{1,0:T(8,128)} %copy-done.8) | copy-start | bytes 3076
  106.3 15.9 %copy-start.11 = (f32[16,16]{1,0:T(8,128)S(1)}, f32[16,16]{1,0:T(8,128)}, u32[]{:S(2)}) copy-start(f32[16,16]{1,0:T(8,128)} %copy-done.10) | copy-start | bytes 3076
  106.3 15.9 %copy-start.24 = (f32[16,16]{1,0:T(8,128)S(1)}, f32[16,16]{1,0:T(8,128)}, u32[]{:S(2)}) copy-start(f32[16,16]{1,0:T(8,128)} %copy-done.23) | copy-start | bytes 3076
  106.4 93.0 %all-reduce.15.cloned.1.call-start = ((), (), s32[]{:S(2)}) async-start(), calls=%async_computation.7 | async-start | bytes 786432 | tf_op jit(solution)/shard_map/psum | solution.py:144
  125.0 109.1 %all-reduce.13.cloned.1.call-start = ((), (), s32[]{:S(2)}) async-start(), calls=%async_computation.6 | async-start | bytes 786432 | tf_op jit(solution)/shard_map/psum | solution.py:147
  234.1 1.6 copy-start.20
  234.1 2.2 copy-start.19
  235.7 1.3 copy-start.5
  (9 other events, 5.9 us)
Sparse Core Ops, SparseCore 0:
  15.5 36.6 all-reduce.8
  77.0 21.4 reduce-scatter.4
  101.2 19.9 reduce-scatter.2
  123.4 35.3 all-reduce.10
  161.9 37.3 all-reduce.14
  201.8 32.2 all-reduce.12
where the time goes:
time: 245 us; the launch traced here: 244 us
  waiting for transfers between devices  148 us (60%)
  blocking collectives  50.3 us (21%)
  between operations  15.2 us (6%)
  other arithmetic  12 us (5%)
  matrix products  10.6 us (4%)
  local copies, waits for them, and re-layouts  8.59 us (4%)
    psum x2, waiting for transfers between devices, from_root(): return lax.psum(jnp.where(mine, x, jnp.zeros_like(x)), axis)  60.9 us
    psum x1, waiting for transfers between devices, on_device(): lax.psum((partial_sums[0], partial_sums[1], partial_sums[2], partial_sums...  34.2 us
    psum x1, waiting for transfers between devices, on_device(): lax.psum((sum_left, sum_right, sum_gate, sum_out, sum_norm_in, sum_norm_m...  21.2 us
    reduce_scatter x1, waiting for transfers between devices, on_device(): lax.psum_scatter(jnp.einsum('ijh,ikh->kjh', grad_product, piece, preferre...  16.5 us
    reduce_scatter x1, waiting for transfers between devices, on_device(): lax.psum_scatter(jnp.einsum('ijh,jkh->kih', grad_product, piece, preferre...  14.8 us
    all_gather x1, blocking collectives, on_device(): lax.all_gather(right.astype(jnp.bfloat16), 'row', axis=1, tiled=True)  14.4 us
    psum x1, blocking collectives, on_device(): lax.psum((sum_left, sum_right, sum_gate, sum_out, sum_norm_in, sum_norm_m...  10.8 us
    all_gather x1, blocking collectives, flip_pair(): lined = lax.all_gather(block, 'col', axis=1, tiled=True)  7.41 us
  transfers between devices with their start and end apart: 6, of which 6 were waited for; matrix products, arithmetic and copies ran while one was open for 6% of the time, Pallas kernels for 0%

commit v1 on v0

v1 whole, which is shorter than its diff:
```python
import functools

import jax
import jax.numpy as jnp
from jax import lax
from jax.experimental import pallas as pl
from jax.experimental.pallas import tpu as pltpu
from jax.sharding import PartitionSpec as P

EPS = 1e-05
MESH = pl.DeviceIdType.MESH
F32 = jnp.float32
BF16 = jnp.bfloat16
EXTRA = 16


def normalize(value, gain, bias):
    centre = value - jnp.mean(value, axis=-1, keepdims=True)
    spread = lax.rsqrt(jnp.mean(centre * centre, axis=-1, keepdims=True) + EPS)
    scaled = centre * spread
    return scaled * gain + bias, scaled, spread


def norm_back(upstream, gain, scaled, spread):
    inner = upstream * gain
    centred = inner - jnp.mean(inner, axis=-1, keepdims=True)
    return spread * (centred - scaled * jnp.mean(inner * scaled, axis=-1, keepdims=True))


def dot(a, b):
    return jnp.dot(a, b, preferred_element_type=F32)


def dot_t(a, b):
    return lax.dot_general(a, b, (((1,), (1,)), ((), ())), preferred_element_type=F32)


def cell_sum(a, b):
    return lax.dot_general(a, b, (((0,), (0,)), ((), ())), preferred_element_type=F32)


def pack_pair(first, second):
    place = lax.broadcasted_iota(jnp.int32, (EXTRA, first.shape[-1]), 0)
    lead_1, lead_2 = first.astype(BF16).astype(F32), second.astype(BF16).astype(F32)
    packed = jnp.where(place == 0, lead_1, 0.0)
    packed = jnp.where(place == 1, lead_2, packed)
    packed = jnp.where(place == 2, first - lead_1, packed)
    packed = jnp.where(place == 3, second - lead_2, packed)
    return packed.astype(BF16)


def unpack_pair(rows):
    return rows[0:1] + rows[2:3], rows[1:2] + rows[3:4]


def kernel(
    n,
    lengths_ref, pair_ref, cot_ref, in_gain_ref, in_bias_ref, left_w_ref, right_w_ref, gate_w_ref,
    mid_gain_ref, mid_bias_ref, out_w_ref,
    result_ref, grad_pair_ref, d_left_ref, d_right_ref, d_gate_ref, d_out_ref, d_in_ref, d_mid_ref,
    left_buf, right_own, right_buf, left_f, right_f, prod_ref, gp_ref,
    gl_out, gl_in, gr_out, gr_in,
    a_src, a_in, a_mid, a_fin, b_src, b_in, b_mid, b_fin,
    l_send, l_recv, r_send, r_recv, gl_send, gl_recv, gr_send, gr_recv,
    a1_send, a1_recv, a2_send, a2_recv, a3_send, a3_recv,
    b1_send, b1_recv, b2_send, b2_recv, b3_send, b3_recv,
):
    block, _, width = pair_ref.shape
    cells = block * block
    row, col = lax.axis_index("row"), lax.axis_index("col")
    everyone = n * n

    def remote(src, dst, send, recv, to_row, to_col):
        return pltpu.make_async_remote_copy(
            src_ref=src, dst_ref=dst, send_sem=send, recv_sem=recv,
            device_id={"row": to_row, "col": to_col}, device_id_type=MESH,
        )

    def peers(body, first=1):
        def step(d, carry):
            body(d)
            return carry

        lax.fori_loop(first, n, step, 0)

    barrier = pltpu.get_barrier_semaphore()

    def greet(d, carry):
        other = lax.rem(row * n + col + d, everyone)
        pl.semaphore_signal(
            barrier, inc=1, device_id={"row": other // n, "col": lax.rem(other, n)}, device_id_type=MESH
        )
        return carry

    lax.fori_loop(1, everyone, greet, 0)

    cell = lax.broadcasted_iota(jnp.int32, (cells, 1), 0)
    count = lengths_ref[0]
    mask = jnp.where(
        (row * block + cell // block < count) & (col * block + cell % block < count), 1.0, 0.0
    ).astype(F32)
    in_gain, in_bias = in_gain_ref[...], in_bias_ref[...]
    normed, scaled_in, spread_in = normalize(
        pair_ref[...].reshape(cells, width).astype(F32), in_gain, in_bias
    )
    normed_b = normed.astype(BF16)

    right_all = dot(normed_b, right_w_ref[...])
    half = right_all.shape[1] // 2
    right_values, right_switch = right_all[:, :half], jax.nn.sigmoid(right_all[:, half:])
    right_gate = mask * right_switch
    right_b = (right_gate * right_values).astype(BF16).reshape(block, block, half)
    right_own[...] = right_b

    @pl.when(row == col)
    def _():
        right_buf[col] = right_b

    pl.semaphore_wait(barrier, everyone - 1)

    def right_copy(d):
        to_row = lax.rem(row + d, n)
        return remote(right_own, right_buf.at[col], r_send.at[d], r_recv.at[col], to_row, row)

    peers(lambda d: right_copy(d).start())

    @pl.when(row != col)
    def _():
        right_copy(0).start()

    left_all = dot(normed_b, left_w_ref[...])
    left_values, left_switch = left_all[:, :half], jax.nn.sigmoid(left_all[:, half:])
    left_gate = mask * left_switch
    left_buf[col] = (left_gate * left_values).astype(BF16).reshape(block, block, half)

    def left_copy(d):
        to_col = lax.rem(col + d, n)
        return remote(left_buf.at[col], left_buf.at[col], l_send.at[d], l_recv.at[col], row, to_col)

    peers(lambda d: left_copy(d).start())

    switch_out = jax.nn.sigmoid(dot(normed_b, gate_w_ref[...]))
    upstream = cot_ref[...].reshape(cells, width).astype(F32)
    grad_update = (upstream * switch_out).astype(BF16)
    grad_mixed = dot_t(grad_update, out_w_ref[...])

    def arrived(buf, recv, slot):
        remote(buf.at[slot], buf.at[slot], recv.at[slot], recv.at[slot], row, col).wait_recv()

    def left_in(d):
        arrived(left_buf, l_recv, lax.rem(col + d, n))

    peers(left_in)
    left_f[...] = left_buf[...].astype(F32)

    def right_in(slot):
        @pl.when((row != col) | (slot != col))
        def _():
            arrived(right_buf, r_recv, slot)

    peers(right_in, 0)
    right_f[...] = right_buf[...].astype(F32)

    def product_row(i, carry):
        near = left_f[:, i]
        rows = []
        for j in range(block):
            rows.append(jnp.sum(jnp.sum(near * right_f[:, j], axis=0), axis=0, keepdims=True))
        prod_ref[i] = jnp.concatenate(rows, axis=0)
        return carry

    lax.fori_loop(0, block, product_row, 0)

    mid_gain = mid_gain_ref[...]
    mixed, scaled_mid, spread_mid = normalize(
        prod_ref[...].reshape(cells, half), mid_gain, mid_bias_ref[...]
    )
    mixed_b = mixed.astype(BF16)
    grad_prod = norm_back(grad_mixed, mid_gain, scaled_mid, spread_mid).astype(BF16).astype(F32)
    gp_ref[...] = grad_prod.reshape(block, block, half)

    def gr_copy(d):
        to_col = lax.rem(col + d, n)
        return remote(gr_out.at[to_col], gr_in.at[row], gr_send.at[d], gr_recv.at[row], col, to_col)

    def gr_block(d):
        at = lax.rem(col + d, n)

        def one(j, carry):
            total = gp_ref[0, pl.ds(j, 1), :] * left_f[at, 0]
            for i in range(1, block):
                total = total + gp_ref[i, pl.ds(j, 1), :] * left_f[at, i]
            gr_out[at, j] = total.astype(BF16)
            return carry

        lax.fori_loop(0, block, one, 0)

    def gr_step(d):
        gr_block(d)
        gr_copy(d).start()

    peers(gr_step)
    gr_block(0)

    @pl.when(row == col)
    def _():
        gr_in[row] = gr_out[col]

    @pl.when(row != col)
    def _():
        gr_copy(0).start()

    def gl_copy(d):
        to_col = lax.rem(col + d, n)
        return remote(gl_out.at[to_col], gl_in.at[col], gl_send.at[d], gl_recv.at[col], row, to_col)

    def gl_block(d, into, slot):
        at = lax.rem(col + d, n)

        def one(i, carry):
            total = gp_ref[i, 0:1, :] * right_f[at, 0]
            for j in range(1, block):
                total = total + gp_ref[i, j : j + 1, :] * right_f[at, j]
            into[slot, i] = total.astype(BF16)
            return carry

        lax.fori_loop(0, block, one, 0)

    def gl_step(d):
        gl_block(d, gl_out, lax.rem(col + d, n))
        gl_copy(d).start()

    peers(gl_step)
    gl_block(0, gl_in, col)

    update = dot(mixed_b, out_w_ref[...])
    result_ref[...] = (switch_out * update).astype(BF16).reshape(block, block, width)
    grad_gate = (upstream * update * switch_out * (1.0 - switch_out)).astype(BF16)

    class Reduce:
        def __init__(self, src, into, mid, fin, sems):
            self.src, self.into, self.mid, self.fin = src, into, mid, fin
            self.s1, self.r1, self.s2, self.r2, self.s3, self.r3 = sems
            self.chunk = src.shape[1] - EXTRA

        def fill(self, parts, first, second):
            per = n // len(parts)
            for at, part in enumerate(parts):
                self.src[at * per : (at + 1) * per, : self.chunk] = part.astype(BF16).reshape(
                    per, self.chunk, part.shape[-1]
                )
            packed = pack_pair(first, second)
            for at in range(n):
                self.src[at, self.chunk :] = packed

        def copy_1(self, d):
            to_col = lax.rem(col + d, n)
            return remote(self.src.at[to_col], self.into.at[col], self.s1.at[d], self.r1.at[col], row, to_col)

        def copy_2(self, d):
            to_row = lax.rem(row + d, n)
            return remote(self.mid.at[row], self.mid.at[row], self.s2.at[d], self.r2.at[row], to_row, col)

        def copy_3(self, d):
            to_col = lax.rem(col + d, n)
            return remote(self.fin.at[col], self.fin.at[col], self.s3.at[d], self.r3.at[col], row, to_col)

        def start_1(self):
            peers(lambda d: self.copy_1(d).start())

        def total(self, buf):
            total = buf[0].astype(F32)
            for slot in range(1, n):
                total = total + buf[slot].astype(F32)
            return total[: self.chunk], unpack_pair(total[self.chunk :])

        def start_2(self):
            self.into[col] = self.src[col]
            peers(lambda d: arrived(self.into, self.r1, lax.rem(col + d, n)))
            body, (first, second) = self.total(self.into)
            self.mid[row, : self.chunk] = body.astype(BF16)
            self.mid[row, self.chunk :] = pack_pair(first, second)
            peers(lambda d: self.copy_2(d).start())

        def start_3(self):
            peers(lambda d: arrived(self.mid, self.r2, lax.rem(row + d, n)))
            body, norms = self.total(self.mid)
            self.fin[col] = body.astype(BF16)
            peers(lambda d: self.copy_3(d).start())
            return norms

        def finish(self, count):
            peers(lambda d: arrived(self.fin, self.r3, lax.rem(col + d, n)))
            per = n // count
            return [
                self.fin[at * per : (at + 1) * per].astype(F32).reshape(per * self.chunk, self.fin.shape[-1])
                for at in range(count)
            ]

        def drain(self):
            peers(lambda d: self.copy_1(d).wait_send())
            peers(lambda d: self.copy_2(d).wait_send())
            peers(lambda d: self.copy_3(d).wait_send())

    early = Reduce(a_src, a_in, a_mid, a_fin, (a1_send, a1_recv, a2_send, a2_recv, a3_send, a3_recv))
    late = Reduce(b_src, b_in, b_mid, b_fin, (b1_send, b1_recv, b2_send, b2_recv, b3_send, b3_recv))

    early.fill(
        [cell_sum(normed_b, grad_gate), cell_sum(mixed_b, grad_update)],
        jnp.sum(grad_mixed * scaled_mid, axis=0, keepdims=True),
        jnp.sum(grad_mixed, axis=0, keepdims=True),
    )
    early.start_1()
    grad_normed = dot_t(grad_gate, gate_w_ref[...])

    def gated_back(total, gate, values, switch):
        first = total * gate
        return first.astype(BF16), (first * values * (1.0 - switch)).astype(BF16)

    def slots(buf):
        total = buf[0].astype(F32)
        for slot in range(1, n):
            total = total + buf[slot].astype(F32)
        return total.reshape(cells, half)

    def gr_arrived(slot):
        @pl.when((row != col) | (slot != row))
        def _():
            arrived(gr_in, gr_recv, slot)

    peers(gr_arrived, 0)
    right_1, right_2 = gated_back(slots(gr_in), right_gate, right_values, right_switch)
    right_w = right_w_ref[...]
    grad_normed = grad_normed + dot_t(right_1, right_w[:, :half]) + dot_t(right_2, right_w[:, half:])

    peers(lambda d: arrived(gl_in, gl_recv, lax.rem(col + d, n)))
    left_1, left_2 = gated_back(slots(gl_in), left_gate, left_values, left_switch)
    left_w = left_w_ref[...]
    grad_normed = grad_normed + dot_t(left_1, left_w[:, :half]) + dot_t(left_2, left_w[:, half:])

    late.fill(
        [cell_sum(normed_b, left_1), cell_sum(normed_b, left_2), cell_sum(normed_b, right_1), cell_sum(normed_b, right_2)],
        jnp.sum(grad_normed * scaled_in, axis=0, keepdims=True),
        jnp.sum(grad_normed, axis=0, keepdims=True),
    )
    late.start_1()
    early.start_2()
    grad_pair_ref[...] = norm_back(grad_normed, in_gain, scaled_in, spread_in).reshape(block, block, width)
    late.start_2()
    norm_mid = early.start_3()
    norm_in = late.start_3()

    factor = 1.0 / (block * n)
    d_in_ref[0:1] = norm_in[0] * factor
    d_in_ref[1:2] = norm_in[1] * factor
    d_mid_ref[0:1] = norm_mid[0] * factor
    d_mid_ref[1:2] = norm_mid[1] * factor
    d_gate, d_out = early.finish(2)
    d_gate_ref[...] = d_gate * factor
    d_out_ref[...] = d_out * factor

    @pl.when(row != col)
    def _():
        right_copy(0).wait_send()
        gr_copy(0).wait_send()

    for copy in (right_copy, left_copy, gr_copy, gl_copy):
        peers(lambda d, copy=copy: copy(d).wait_send())
    parts = late.finish(4)
    d_left_ref[:, :half] = parts[0] * factor
    d_left_ref[:, half:] = parts[1] * factor
    d_right_ref[:, :half] = parts[2] * factor
    d_right_ref[:, half:] = parts[3] * factor
    early.drain()
    late.drain()


def solution(mesh):
    n = mesh.shape["row"]
    assert mesh.shape["col"] == n and n % 4 == 0

    def on_device(
        pair, cotangent, lengths, in_gain, in_bias, left_w, right_w, gate_w, mid_gain, mid_bias, out_w
    ):
        block, _, width = pair.shape
        half = left_w.shape[1] // 2
        vmem = pl.BlockSpec(memory_space=pltpu.VMEM)
        smem = pl.BlockSpec(memory_space=pltpu.SMEM)

        def blocks(dtype, *lead):
            return pltpu.VMEM(lead + (block, block, half), dtype)

        def reduce_bufs(rows):
            chunk = rows // n
            return [
                pltpu.VMEM((n, chunk + EXTRA, half), BF16),
                pltpu.VMEM((n, chunk + EXTRA, half), BF16),
                pltpu.VMEM((n, chunk + EXTRA, half), BF16),
                pltpu.VMEM((n, chunk, half), BF16),
            ]

        shape = jax.ShapeDtypeStruct
        return pl.pallas_call(
            functools.partial(kernel, n),
            out_shape=(
                shape(pair.shape, BF16),
                shape(pair.shape, F32),
                shape(left_w.shape, F32),
                shape(right_w.shape, F32),
                shape(gate_w.shape, F32),
                shape(out_w.shape, F32),
                shape((2, width), F32),
                shape((2, half), F32),
            ),
            in_specs=[smem] + [vmem] * 10,
            out_specs=[vmem] * 8,
            scratch_shapes=[
                blocks(BF16, n), blocks(BF16), blocks(BF16, n), blocks(F32, n), blocks(F32, n),
                blocks(F32), blocks(F32),
                blocks(BF16, n), blocks(BF16, n), blocks(BF16, n), blocks(BF16, n),
                *reduce_bufs(gate_w.shape[0] + out_w.shape[0]),
                *reduce_bufs(2 * (left_w.shape[0] + right_w.shape[0])),
            ]
            + [pltpu.SemaphoreType.DMA((n,))] * 20,
            compiler_params=pltpu.CompilerParams(
                collective_id=0, has_side_effects=True, vmem_limit_bytes=48 * 1024 * 1024
            ),
        )(
            lengths, pair, cotangent, in_gain.reshape(1, -1), in_bias.reshape(1, -1), left_w, right_w, gate_w,
            mid_gain.reshape(1, -1), mid_bias.reshape(1, -1), out_w,
        )

    cells = P(("grp", "row"), "col", None)
    return jax.shard_map(
        on_device,
        mesh=mesh,
        in_specs=(cells, cells, P("grp")) + (P(),) * 8,
        out_specs=(cells, cells) + (P("grp", None),) * 6,
        check_vma=False,
    )
```

time: 245 us -> 51.9 us (0.21)
  waiting for transfers between devices: 148 us -> 0 us
  blocking collectives: 50.3 us -> 0 us
  Pallas kernels: 0 us -> 39.6 us
  between operations: 15.2 us -> 1.33 us
  other arithmetic: 12 us -> 0 us
  matrix products: 10.6 us -> 0 us
    psum x4 -> x0, waiting for transfers between devices: 116 us -> none  [the longest x2 60.9 us: from_root(): return lax.psum(jnp.where(mine, x, jnp.zeros_like(x)), axis)]
    pallas_call x0 -> x1, Pallas kernels: none -> 39.6 us  [on_device(): pl.pallas_call(functools.partial(kernel, n), out_shape=(shape(pair.shape,...]
    all_gather x4 -> x0, blocking collectives: 33.5 us -> none  [the longest x1 14.4 us: on_device(): lax.all_gather(right.astype(jnp.bfloat16), 'row', axis=1, tiled=True)]
    reduce_scatter x2 -> x0, waiting for transfers between devices: 31.2 us -> none  [the longest x1 16.5 us: on_device(): lax.psum_scatter(jnp.einsum('ijh,ikh->kjh', grad_product, piece, preferre...]
    psum x2 -> x0, blocking collectives: 16.8 us -> none  [the longest x1 10.8 us: on_device(): lax.psum((sum_left, sum_right, sum_gate, sum_out, sum_norm_in, sum_norm_m...]
    dot_general x15 -> x0, matrix products: 10.6 us -> none  [the longest x4 4.71 us: cell_sum(): jnp.einsum('ijc,ijh->ch', first, second, preferred_element_type=jnp.float32)]
    unnamed x70 -> x28, local copies, waits for them, and re-layouts: 4.33 us -> 10.5 us
    mul x8 -> x0, other arithmetic: 5.6 us -> none  [the longest x1 1.6 us: on_device(): totals[0] * factor]
  transfers between devices with their start and end apart: 6 -> 0, of which waited for: 6 -> 0; matrix products, arithmetic and copies ran while one was open for 6% -> 0% of each run, Pallas kernels for 0% -> 0%
where the time goes in v1:
time: 51.9 us; the launch traced here: 51.4 us
  Pallas kernels  39.6 us (76%)
  local copies, waits for them, and re-layouts  10.5 us (20%)
  between operations  1.33 us (3%)
    pallas_call x1, Pallas kernels, on_device(): pl.pallas_call(functools.partial(kernel, n), out_shape=(shape(pair.shape,...  39.6 us
    unnamed x28, local copies, waits for them, and re-layouts  10.5 us

profile of v1, /device:TPU:0, one launch (start us, length us, event | category | flops | bytes accessed | tf_op | source)
XLA Modules:
  0.0 51.4 jit_solution(15495661441282931945)
XLA Ops:
  1.3 0.0 copy-start.9
  1.3 0.0 copy-start.6
  1.3 0.0 copy-start.7
  1.3 0.0 copy-start.8
  1.3 0.6 %copy-done.9 = f32[128]{0:T(128)S(1)} copy-done((f32[128]{0:T(128)S(1)}, f32[128]{0:T(128)}, u32[]{:S(2)}) %copy-start.9) | copy-done | bytes 536
  1.9 0.0 copy-done.6
  2.0 0.0 copy-done.7
  2.0 0.0 copy-done.8
  2.0 0.0 copy-start
  2.0 0.8 %copy-done = bf16[16,16,128]{2,1,0:T(8,128)(2,1)S(1)} copy-done((bf16[16,16,128]{2,1,0:T(8,128)(2,1)S(1)}, bf16[16,16,128]{2,1,0:T(8,128)(2,1)}, u32[]{:S(2)}) %copy-start) | copy-done | bytes 65560
  2.8 0.0 copy-start.1
  2.8 0.8 %copy-done.1 = bf16[16,16,128]{2,1,0:T(8,128)(2,1)S(1)} copy-done((bf16[16,16,128]{2,1,0:T(8,128)(2,1)S(1)}, bf16[16,16,128]{2,1,0:T(8,128)(2,1)}, u32[]{:S(2)}) %copy-start.1) | copy-done | bytes 65560
  3.7 0.0 copy-start.2
  3.7 0.8 %copy-done.2 = bf16[128,256]{1,0:T(8,128)(2,1)S(1)} copy-done((bf16[128,256]{1,0:T(8,128)(2,1)S(1)}, bf16[128,256]{1,0:T(8,128)(2,1)}, u32[]{:S(2)}) %copy-start.2) | copy-done | bytes 65560
  4.5 0.0 copy-start.3
  4.5 0.8 %copy-done.3 = bf16[128,256]{1,0:T(8,128)(2,1)S(1)} copy-done((bf16[128,256]{1,0:T(8,128)(2,1)S(1)}, bf16[128,256]{1,0:T(8,128)(2,1)}, u32[]{:S(2)}) %copy-start.3) | copy-done | bytes 65560
  5.3 0.0 copy-start.4
  5.3 0.8 %copy-done.4 = bf16[128,128]{1,0:T(8,128)(2,1)S(1)} copy-done((bf16[128,128]{1,0:T(8,128)(2,1)S(1)}, bf16[128,128]{1,0:T(8,128)(2,1)}, u32[]{:S(2)}) %copy-start.4) | copy-done | bytes 32792
  6.1 0.0 copy-start.5
  6.1 0.8 %copy-done.5 = bf16[128,128]{1,0:T(8,128)(2,1)S(1)} copy-done((bf16[128,128]{1,0:T(8,128)(2,1)S(1)}, bf16[128,128]{1,0:T(8,128)(2,1)}, u32[]{:S(2)}) %copy-start.5) | copy-done | bytes 32792
  6.9 39.6 %shard_map.170 = (bf16[16,16,128]{2,1,0:T(8,128)(2,1)S(1)}, f32[16,16,128]{2,1,0:T(8,128)S(1)}, f32[128,256]{1,0:T(8,128)S(1)}, f32[128,256]{1,0:T(8,128)S(1)}, ...) custom-call(s32[1]{0:T(128)S(6)} %copy.27.lengths_ref, ...), custom_call_target="tpu_custom_call" | custom-call | tf_op jit(solution)/shard_map/pallas_call | solution.py:403
  46.5 0.6 %copy.28 = bf16[16,16,128]{2,1,0:T(8,128)(2,1)} copy(bf16[16,16,128]{2,1,0:T(8,128)(2,1)S(1)} %get-tuple-element.16) | data formatting | bytes 131072
  47.1 0.7 %copy.29 = f32[16,16,128]{2,1,0:T(8,128)} copy(f32[16,16,128]{2,1,0:T(8,128)S(1)} %get-tuple-element.17) | data formatting | bytes 262144
  47.7 0.7 %copy.30 = f32[128,256]{1,0:T(8,128)} copy(f32[128,256]{1,0:T(8,128)S(1)} %get-tuple-element.18) | data formatting | bytes 262144
  48.4 0.7 %copy.31 = f32[128,256]{1,0:T(8,128)} copy(f32[128,256]{1,0:T(8,128)S(1)} %get-tuple-element.19) | data formatting | bytes 262144
  49.1 0.6 %copy.32 = f32[128,128]{1,0:T(8,128)} copy(f32[128,128]{1,0:T(8,128)S(1)} %get-tuple-element.20) | data formatting | bytes 131072
  49.7 0.6 %copy.33 = f32[128,128]{1,0:T(8,128)} copy(f32[128,128]{1,0:T(8,128)S(1)} %get-tuple-element.21) | data formatting | bytes 131072
  50.3 0.6 %copy.34 = f32[2,128]{1,0:T(2,128)} copy(f32[2,128]{1,0:T(2,128)S(1)} %get-tuple-element.22) | data formatting | bytes 2048
  50.9 0.6 %copy.35 = f32[2,128]{1,0:T(2,128)} copy(f32[2,128]{1,0:T(2,128)S(1)} %get-tuple-element.23) | data formatting | bytes 2048
Async XLA Ops:
  1.3 0.7 %copy-start.9 = (f32[128]{0:T(128)S(1)}, f32[128]{0:T(128)}, u32[]{:S(2)}) copy-start(f32[128]{0:T(128)} %param.20) | copy-start | bytes 1540
  1.3 0.7 %copy-start.6 = (f32[128]{0:T(128)S(1)}, f32[128]{0:T(128)}, u32[]{:S(2)}) copy-start(f32[128]{0:T(128)} %param.14) | copy-start | bytes 1540
  1.3 0.7 %copy-start.7 = (f32[128]{0:T(128)S(1)}, f32[128]{0:T(128)}, u32[]{:S(2)}) copy-start(f32[128]{0:T(128)} %param.15) | copy-start | bytes 1540
  1.3 0.7 %copy-start.8 = (f32[128]{0:T(128)S(1)}, f32[128]{0:T(128)}, u32[]{:S(2)}) copy-start(f32[128]{0:T(128)} %param.19) | copy-start | bytes 1540
  2.0 0.8 %copy-start = (bf16[16,16,128]{2,1,0:T(8,128)(2,1)S(1)}, bf16[16,16,128]{2,1,0:T(8,128)(2,1)}, u32[]{:S(2)}) copy-start(bf16[16,16,128]{2,1,0:T(8,128)(2,1)} %pair_ref.1) | copy-start | bytes 196612
  2.8 0.8 %copy-start.1 = (bf16[16,16,128]{2,1,0:T(8,128)(2,1)S(1)}, bf16[16,16,128]{2,1,0:T(8,128)(2,1)}, u32[]{:S(2)}) copy-start(bf16[16,16,128]{2,1,0:T(8,128)(2,1)} %cot_ref.1) | copy-start | bytes 196612
  3.7 0.8 %copy-start.2 = (bf16[128,256]{1,0:T(8,128)(2,1)S(1)}, bf16[128,256]{1,0:T(8,128)(2,1)}, u32[]{:S(2)}) copy-start(bf16[128,256]{1,0:T(8,128)(2,1)} %left_w_ref.1) | copy-start | bytes 196612
  4.5 0.8 %copy-start.3 = (bf16[128,256]{1,0:T(8,128)(2,1)S(1)}, bf16[128,256]{1,0:T(8,128)(2,1)}, u32[]{:S(2)}) copy-start(bf16[128,256]{1,0:T(8,128)(2,1)} %right_w_ref.1) | copy-start | bytes 196612
  5.3 0.8 %copy-start.4 = (bf16[128,128]{1,0:T(8,128)(2,1)S(1)}, bf16[128,128]{1,0:T(8,128)(2,1)}, u32[]{:S(2)}) copy-start(bf16[128,128]{1,0:T(8,128)(2,1)} %gate_w_ref.1) | copy-start | bytes 98308
  6.1 0.8 %copy-start.5 = (bf16[128,128]{1,0:T(8,128)(2,1)S(1)}, bf16[128,128]{1,0:T(8,128)(2,1)}, u32[]{:S(2)}) copy-start(bf16[128,128]{1,0:T(8,128)(2,1)} %out_w_ref.1) | copy-start | bytes 98308

commit v2 on v1

v2 whole, which is shorter than its diff:
```python
import functools

import jax
import jax.numpy as jnp
from jax import lax
from jax.experimental import pallas as pl
from jax.experimental.pallas import tpu as pltpu
from jax.sharding import PartitionSpec as P

EPS = 1e-05
MESH = pl.DeviceIdType.MESH
F32 = jnp.float32
BF16 = jnp.bfloat16
EXTRA = 16


def normalize(value, gain, bias):
    centre = value - jnp.mean(value, axis=-1, keepdims=True)
    spread = lax.rsqrt(jnp.mean(centre * centre, axis=-1, keepdims=True) + EPS)
    scaled = centre * spread
    return scaled * gain + bias, scaled, spread


def norm_back(upstream, gain, scaled, spread):
    inner = upstream * gain
    centred = inner - jnp.mean(inner, axis=-1, keepdims=True)
    return spread * (centred - scaled * jnp.mean(inner * scaled, axis=-1, keepdims=True))


def dot(a, b):
    return jnp.dot(a, b, preferred_element_type=F32)


def dot_t(a, b):
    return lax.dot_general(a, b, (((1,), (1,)), ((), ())), preferred_element_type=F32)


def cell_sum(a, b):
    return lax.dot_general(a, b, (((0,), (0,)), ((), ())), preferred_element_type=F32)


def pack_pair(first, second):
    place = lax.broadcasted_iota(jnp.int32, (EXTRA, first.shape[-1]), 0)
    lead_1, lead_2 = first.astype(BF16).astype(F32), second.astype(BF16).astype(F32)
    packed = jnp.where(place == 0, lead_1, 0.0)
    packed = jnp.where(place == 1, lead_2, packed)
    packed = jnp.where(place == 2, first - lead_1, packed)
    packed = jnp.where(place == 3, second - lead_2, packed)
    return packed.astype(BF16)


def unpack_pair(rows):
    return rows[0:1] + rows[2:3], rows[1:2] + rows[3:4]


def kernel(
    n,
    lengths_ref, pair_hbm, cot_hbm, in_gain_hbm, in_bias_hbm, left_w_hbm, right_w_hbm, gate_w_hbm,
    mid_gain_hbm, mid_bias_hbm, out_w_hbm,
    result_ref, grad_pair_ref, d_left_ref, d_right_ref, d_gate_ref, d_out_ref, d_in_ref, d_mid_ref,
    pair_ref, cot_ref, in_gain_ref, in_bias_ref, left_w_ref, right_w_ref, gate_w_ref,
    mid_gain_ref, mid_bias_ref, out_w_ref,
    left_f, right_buf, right_f, pp_out, pp_in, gp_buf, gp_f, gl_f, gr_out, gr_in,
    a_src, a_in, a_mid, a_fin, b_src, b_in, b_mid, b_fin,
    load_sem,
    r_send, r_recv, pp_send, pp_recv, gp_send, gp_recv, gr_send, gr_recv,
    a1_send, a1_recv, a2_send, a2_recv, a3_send, a3_recv,
    b1_send, b1_recv, b2_send, b2_recv, b3_send, b3_recv,
):
    block, _, width = pair_ref.shape
    half = out_w_ref.shape[0]
    cells = block * block
    row, col = lax.axis_index("row"), lax.axis_index("col")
    everyone = n * n

    def remote(src, dst, send, recv, to_row, to_col):
        return pltpu.make_async_remote_copy(
            src_ref=src, dst_ref=dst, send_sem=send, recv_sem=recv,
            device_id={"row": to_row, "col": to_col}, device_id_type=MESH,
        )

    def peers(body, first=1):
        def step(d, carry):
            body(d)
            return carry

        lax.fori_loop(first, n, step, 0)

    def arrived(buf, recv, slot):
        remote(buf.at[slot], buf.at[slot], recv.at[slot], recv.at[slot], row, col).wait_recv()

    loads = [
        pltpu.make_async_copy(src, dst, load_sem.at[at])
        for at, (src, dst) in enumerate(
            (
                (pair_hbm, pair_ref), (right_w_hbm, right_w_ref), (in_gain_hbm, in_gain_ref),
                (in_bias_hbm, in_bias_ref), (left_w_hbm, left_w_ref), (gate_w_hbm, gate_w_ref),
                (cot_hbm, cot_ref), (out_w_hbm, out_w_ref), (mid_gain_hbm, mid_gain_ref),
                (mid_bias_hbm, mid_bias_ref),
            )
        )
    ]
    for load in loads:
        load.start()
    barrier = pltpu.get_barrier_semaphore()

    def greet(d, carry):
        other = lax.rem(row * n + col + d, everyone)
        pl.semaphore_signal(
            barrier, inc=1, device_id={"row": other // n, "col": lax.rem(other, n)}, device_id_type=MESH
        )
        return carry

    lax.fori_loop(1, everyone, greet, 0)

    cell = lax.broadcasted_iota(jnp.int32, (cells, 1), 0)
    count = lengths_ref[0]
    mask = jnp.where(
        (row * block + cell // block < count) & (col * block + cell % block < count), 1.0, 0.0
    ).astype(F32)
    for load in loads[:4]:
        load.wait()
    in_gain, in_bias = in_gain_ref[...], in_bias_ref[...]
    normed, scaled_in, spread_in = normalize(
        pair_ref[...].reshape(cells, width).astype(F32), in_gain, in_bias
    )
    normed_b = normed.astype(BF16)

    right_all = dot(normed_b, right_w_ref[...])
    right_values, right_switch = right_all[:, :half], jax.nn.sigmoid(right_all[:, half:])
    right_gate = mask * right_switch
    right_buf[row] = (right_gate * right_values).astype(BF16).reshape(block, block, half)
    pl.semaphore_wait(barrier, everyone - 1)

    def right_copy(d):
        return remote(
            right_buf.at[row], right_buf.at[row], r_send.at[d], r_recv.at[row], lax.rem(row + d, n), col
        )

    peers(lambda d: right_copy(d).start())

    for load in loads[4:]:
        load.wait()
    left_all = dot(normed_b, left_w_ref[...])
    left_values, left_switch = left_all[:, :half], jax.nn.sigmoid(left_all[:, half:])
    left_gate = mask * left_switch
    left_f[...] = (left_gate * left_values).astype(BF16).astype(F32).reshape(block, block, half)

    switch_out = jax.nn.sigmoid(dot(normed_b, gate_w_ref[...]))
    upstream = cot_ref[...].reshape(cells, width).astype(F32)
    grad_update = (upstream * switch_out).astype(BF16)
    grad_mixed = dot_t(grad_update, out_w_ref[...])

    def pp_copy(to_col):
        return remote(pp_out.at[to_col], pp_in.at[col], pp_send.at[to_col], pp_recv.at[col], row, to_col)

    def product_block(d, wait):
        at = lax.rem(row + d, n)
        if wait:
            arrived(right_buf, r_recv, at)
        right_f[at] = right_buf[at].astype(F32)

        def one(i, carry):
            near = left_f[i]
            rows = [jnp.sum(near * right_f[at, j], axis=0, keepdims=True) for j in range(block)]
            pp_out[at, i] = jnp.concatenate(rows, axis=0).astype(BF16)
            return carry

        lax.fori_loop(0, block, one, 0)

        @pl.when(at != col)
        def _():
            pp_copy(at).start()

    product_block(0, False)
    peers(lambda d: product_block(d, True))

    def summed(own, buf, first):
        def step(d, total):
            slot = lax.rem(first + d, n)
            return total + buf[slot].astype(F32)

        return lax.fori_loop(1, n, step, own.astype(F32)).reshape(cells, half)

    peers(lambda d: arrived(pp_in, pp_recv, lax.rem(col + d, n)))
    product = summed(pp_out[col], pp_in, col)
    mid_gain = mid_gain_ref[...]
    mixed, scaled_mid, spread_mid = normalize(product, mid_gain, mid_bias_ref[...])
    grad_prod = norm_back(grad_mixed, mid_gain, scaled_mid, spread_mid)
    gp_buf[col] = grad_prod.astype(BF16).reshape(block, block, half)

    def gp_copy(d):
        return remote(
            gp_buf.at[col], gp_buf.at[col], gp_send.at[d], gp_recv.at[col], row, lax.rem(col + d, n)
        )

    peers(lambda d: gp_copy(d).start())

    def gr_copy(to_row):
        return remote(gr_out.at[to_row], gr_in.at[row], gr_send.at[to_row], gr_recv.at[row], to_row, col)

    def gr_block(d, wait):
        at = lax.rem(col + d, n)
        if wait:
            arrived(gp_buf, gp_recv, at)
        gp_f[at] = gp_buf[at].astype(F32)

        def one(j, carry):
            total = gp_f[at, 0, pl.ds(j, 1), :] * left_f[0]
            for i in range(1, block):
                total = total + gp_f[at, i, pl.ds(j, 1), :] * left_f[i]
            gr_out[at, j] = total.astype(BF16)
            return carry

        lax.fori_loop(0, block, one, 0)

        @pl.when(at != row)
        def _():
            gr_copy(at).start()

    gr_block(0, False)

    mixed_b = mixed.astype(BF16)
    update = dot(mixed_b, out_w_ref[...])
    result_ref[...] = (switch_out * update).astype(BF16).reshape(block, block, width)
    grad_gate = (upstream * update * switch_out * (1.0 - switch_out)).astype(BF16)

    peers(lambda d: gr_block(d, True))

    def gl_row(i, carry):
        def step(at, total):
            for j in range(block):
                total = total + gp_f[at, i, j : j + 1, :] * right_f[at, j]
            return total

        gl_f[i] = lax.fori_loop(0, n, step, jnp.zeros((block, half), F32))
        return carry

    lax.fori_loop(0, block, gl_row, 0)

    def gated_back(total, gate, values, switch):
        first = total * gate
        return first.astype(BF16), (first * values * (1.0 - switch)).astype(BF16)

    left_1, left_2 = gated_back(gl_f[...].reshape(cells, half), left_gate, left_values, left_switch)

    class Reduce:
        def __init__(self, src, into, mid, fin, sems):
            self.src, self.into, self.mid, self.fin = src, into, mid, fin
            self.s1, self.r1, self.s2, self.r2, self.s3, self.r3 = sems
            self.chunk = src.shape[1] - EXTRA

        def fill(self, parts, first, second):
            per = n // len(parts)
            for at, part in enumerate(parts):
                self.src[at * per : (at + 1) * per, : self.chunk] = part.astype(BF16).reshape(
                    per, self.chunk, part.shape[-1]
                )
            packed = pack_pair(first, second)
            for at in range(n):
                self.src[at, self.chunk :] = packed

        def copy_1(self, d):
            to_col = lax.rem(col + d, n)
            return remote(self.src.at[to_col], self.into.at[col], self.s1.at[d], self.r1.at[col], row, to_col)

        def copy_2(self, d):
            to_row = lax.rem(row + d, n)
            return remote(self.mid.at[row], self.mid.at[row], self.s2.at[d], self.r2.at[row], to_row, col)

        def copy_3(self, d):
            to_col = lax.rem(col + d, n)
            return remote(self.fin.at[col], self.fin.at[col], self.s3.at[d], self.r3.at[col], row, to_col)

        def start_1(self):
            peers(lambda d: self.copy_1(d).start())

        def total(self, buf):
            total = buf[0].astype(F32)
            for slot in range(1, n):
                total = total + buf[slot].astype(F32)
            return total[: self.chunk], unpack_pair(total[self.chunk :])

        def start_2(self):
            self.into[col] = self.src[col]
            peers(lambda d: arrived(self.into, self.r1, lax.rem(col + d, n)))
            body, (first, second) = self.total(self.into)
            self.mid[row, : self.chunk] = body.astype(BF16)
            self.mid[row, self.chunk :] = pack_pair(first, second)
            peers(lambda d: self.copy_2(d).start())

        def start_3(self):
            peers(lambda d: arrived(self.mid, self.r2, lax.rem(row + d, n)))
            body, norms = self.total(self.mid)
            self.fin[col] = body.astype(BF16)
            peers(lambda d: self.copy_3(d).start())
            return norms

        def finish(self, count):
            peers(lambda d: arrived(self.fin, self.r3, lax.rem(col + d, n)))
            per = n // count
            return [
                self.fin[at * per : (at + 1) * per].astype(F32).reshape(per * self.chunk, self.fin.shape[-1])
                for at in range(count)
            ]

        def drain(self):
            peers(lambda d: self.copy_1(d).wait_send())
            peers(lambda d: self.copy_2(d).wait_send())
            peers(lambda d: self.copy_3(d).wait_send())

    early = Reduce(a_src, a_in, a_mid, a_fin, (a1_send, a1_recv, a2_send, a2_recv, a3_send, a3_recv))
    late = Reduce(b_src, b_in, b_mid, b_fin, (b1_send, b1_recv, b2_send, b2_recv, b3_send, b3_recv))

    early.fill(
        [
            cell_sum(normed_b, grad_gate), cell_sum(mixed_b, grad_update),
            cell_sum(normed_b, left_1), cell_sum(normed_b, left_2),
        ],
        jnp.sum(grad_mixed * scaled_mid, axis=0, keepdims=True),
        jnp.sum(grad_mixed, axis=0, keepdims=True),
    )
    early.start_1()
    left_w, right_w = left_w_ref[...], right_w_ref[...]
    grad_normed = dot_t(grad_gate, gate_w_ref[...])
    grad_normed = grad_normed + dot_t(left_1, left_w[:, :half]) + dot_t(left_2, left_w[:, half:])

    peers(lambda d: arrived(gr_in, gr_recv, lax.rem(row + d, n)))
    grad_right = summed(gr_out[row], gr_in, row)
    right_1, right_2 = gated_back(grad_right, right_gate, right_values, right_switch)
    grad_normed = grad_normed + dot_t(right_1, right_w[:, :half]) + dot_t(right_2, right_w[:, half:])

    late.fill(
        [cell_sum(normed_b, right_1), cell_sum(normed_b, right_2)],
        jnp.sum(grad_normed * scaled_in, axis=0, keepdims=True),
        jnp.sum(grad_normed, axis=0, keepdims=True),
    )
    late.start_1()
    early.start_2()
    grad_pair_ref[...] = norm_back(grad_normed, in_gain, scaled_in, spread_in).reshape(block, block, width)
    late.start_2()
    norm_mid = early.start_3()
    norm_in = late.start_3()

    factor = 1.0 / (block * n)
    d_in_ref[0:1] = norm_in[0] * factor
    d_in_ref[1:2] = norm_in[1] * factor
    d_mid_ref[0:1] = norm_mid[0] * factor
    d_mid_ref[1:2] = norm_mid[1] * factor
    parts = early.finish(4)
    d_gate_ref[...] = parts[0] * factor
    d_out_ref[...] = parts[1] * factor
    d_left_ref[:, :half] = parts[2] * factor
    d_left_ref[:, half:] = parts[3] * factor

    for copy in (right_copy, gp_copy):
        peers(lambda d, copy=copy: copy(d).wait_send())
    peers(lambda d: pp_copy(lax.rem(col + d, n)).wait_send())
    peers(lambda d: gr_copy(lax.rem(row + d, n)).wait_send())
    parts = late.finish(2)
    d_right_ref[:, :half] = parts[0] * factor
    d_right_ref[:, half:] = parts[1] * factor
    early.drain()
    late.drain()


def write_out(*refs):
    sem = refs[-1]
    count = len(refs) // 2
    copies = [
        pltpu.make_async_copy(src, dst, sem.at[at])
        for at, (src, dst) in enumerate(zip(refs[:count], refs[count : 2 * count]))
    ]
    for copy in copies:
        copy.start()
    for copy in copies:
        copy.wait()


def solution(mesh):
    n = mesh.shape["row"]
    assert mesh.shape["col"] == n and n % 4 == 0

    def on_device(
        pair, cotangent, lengths, in_gain, in_bias, left_w, right_w, gate_w, mid_gain, mid_bias, out_w
    ):
        block, _, width = pair.shape
        half = left_w.shape[1] // 2
        vmem = pl.BlockSpec(memory_space=pltpu.VMEM)
        smem = pl.BlockSpec(memory_space=pltpu.SMEM)
        hbm = pl.BlockSpec(memory_space=pltpu.HBM)
        operands = [
            pair, cotangent, in_gain.reshape(1, -1), in_bias.reshape(1, -1), left_w, right_w, gate_w,
            mid_gain.reshape(1, -1), mid_bias.reshape(1, -1), out_w,
        ]

        def blocks(dtype, *lead):
            return pltpu.VMEM(lead + (block, block, half), dtype)

        def reduce_bufs(rows):
            chunk = rows // n
            return [
                pltpu.VMEM((n, chunk + EXTRA, half), BF16),
                pltpu.VMEM((n, chunk + EXTRA, half), BF16),
                pltpu.VMEM((n, chunk + EXTRA, half), BF16),
                pltpu.VMEM((n, chunk, half), BF16),
            ]

        shape = jax.ShapeDtypeStruct
        out_shape = (
            shape(pair.shape, BF16),
            shape(pair.shape, F32),
            shape(left_w.shape, F32),
            shape(right_w.shape, F32),
            shape(gate_w.shape, F32),
            shape(out_w.shape, F32),
            shape((2, width), F32),
            shape((2, half), F32),
        )
        outs = pl.pallas_call(
            functools.partial(kernel, n),
            out_shape=out_shape,
            in_specs=[smem] + [hbm] * 10,
            out_specs=[vmem] * 8,
            scratch_shapes=[
                *[pltpu.VMEM(x.shape, x.dtype) for x in operands],
                blocks(F32), blocks(BF16, n), blocks(F32, n), blocks(BF16, n), blocks(BF16, n),
                blocks(BF16, n), blocks(F32, n), blocks(F32), blocks(BF16, n), blocks(BF16, n),
                *reduce_bufs(gate_w.shape[0] + out_w.shape[0] + 2 * left_w.shape[0]),
                *reduce_bufs(2 * right_w.shape[0]),
                pltpu.SemaphoreType.DMA((10,)),
            ]
            + [pltpu.SemaphoreType.DMA((n,))] * 20,
            compiler_params=pltpu.CompilerParams(
                collective_id=0, has_side_effects=True, vmem_limit_bytes=63 * 1024 * 1024
            ),
        )(lengths, *operands)
        return pl.pallas_call(
            write_out,
            out_shape=out_shape,
            in_specs=[vmem] * 8,
            out_specs=[hbm] * 8,
            scratch_shapes=[pltpu.SemaphoreType.DMA((8,))],
        )(*outs)

    cells = P(("grp", "row"), "col", None)
    return jax.shard_map(
        on_device,
        mesh=mesh,
        in_specs=(cells, cells, P("grp")) + (P(),) * 8,
        out_specs=(cells, cells) + (P("grp", None),) * 6,
        check_vma=False,
    )
```

time: 51.9 us -> 45.4 us (0.87)
  local copies, waits for them, and re-layouts: 10.5 us -> 0 us
  Pallas kernels: 39.6 us -> 43.9 us
    unnamed x28 -> x0, local copies, waits for them, and re-layouts: 10.5 us -> none
    pallas_call x1 -> x2, Pallas kernels: 39.6 us -> 43.9 us  [the longest x1 41.9 us: on_device(): pl.pallas_call(functools.partial(kernel, n), out_shape=out_shape, in_spec...]
where the time goes in v2:
time: 45.4 us; the launch traced here: 45.2 us
  Pallas kernels  43.9 us (97%)
  between operations  1.29 us (3%)
    pallas_call x1, Pallas kernels, on_device(): pl.pallas_call(functools.partial(kernel, n), out_shape=out_shape, in_spec...  41.9 us
    pallas_call x1, Pallas kernels, on_device(): pl.pallas_call(write_out, out_shape=out_shape, in_specs=[vmem] * 8, out_s...  1.98 us

profile of v2, /device:TPU:0, one launch (start us, length us, event | category | flops | bytes accessed | tf_op | source)
XLA Modules:
  0.0 45.2 jit_solution(10419187148902282049)
XLA Ops:
  1.3 41.9 %shard_map.170 = (bf16[16,16,128]{2,1,0:T(8,128)(2,1)}, f32[16,16,128]{2,1,0:T(8,128)}, f32[128,256]{1,0:T(8,128)}, f32[128,256]{1,0:T(8,128)}, f32[128,128]{1,0...) custom-call(s32[1]{0:T(128)S(6)} %copy.19.lengths_ref, bf16[16,16,128]{2,1,0:T(8,128)(2,1)} %pair_hbm.1, ...), custom_call_target="tpu_custom_call" | custom-call | tf_op jit(solution)/shard_map/pallas_call | solution.py:420
  43.2 2.0 %shard_map.171 = (bf16[16,16,128]{2,1,0:T(8,128)(2,1)}, f32[16,16,128]{2,1,0:T(8,128)}, f32[128,256]{1,0:T(8,128)}, f32[128,256]{1,0:T(8,128)}, f32[128,128]{1,0...) custom-call(bf16[16,16,128]{2,1,0:T(8,128)(2,1)} %get-tuple-element.16.refs_0_, ...), custom_call_target="tpu_custom_call" | custom-call | tf_op jit(solution)/shard_map/pallas_call | solution.py:438

commit v3 on v2

v3 whole, which is shorter than its diff:
```python
import functools

import jax
import jax.numpy as jnp
from jax import lax
from jax.experimental import pallas as pl
from jax.experimental.pallas import tpu as pltpu
from jax.sharding import PartitionSpec as P

EPS = 1e-05
MESH = pl.DeviceIdType.MESH
F32 = jnp.float32
BF16 = jnp.bfloat16
ROWS = 16


def normalize(value, gain, bias):
    centre = value - jnp.mean(value, axis=-1, keepdims=True)
    spread = lax.rsqrt(jnp.mean(centre * centre, axis=-1, keepdims=True) + EPS)
    scaled = centre * spread
    return scaled * gain + bias, scaled, spread


def norm_back(upstream, gain, scaled, spread):
    inner = upstream * gain
    centred = inner - jnp.mean(inner, axis=-1, keepdims=True)
    return spread * (centred - scaled * jnp.mean(inner * scaled, axis=-1, keepdims=True))


def dot(a, b):
    return jnp.dot(a, b, preferred_element_type=F32)


def dot_t(a, b):
    return lax.dot_general(a, b, (((1,), (1,)), ((), ())), preferred_element_type=F32)


def cell_sum(a, b):
    return lax.dot_general(a, b, (((0,), (0,)), ((), ())), preferred_element_type=F32)


def kernel(
    n,
    lengths_ref, pair_hbm, cot_hbm, in_gain_hbm, in_bias_hbm, left_w_hbm, right_w_hbm, gate_w_hbm,
    mid_gain_hbm, mid_bias_hbm, out_w_hbm,
    result_ref, grad_pair_ref, d_left_ref, d_right_ref, d_gate_ref, d_out_ref, d_in_ref, d_mid_ref,
    pair_ref, cot_ref, in_gain_ref, in_bias_ref, left_w_ref, right_w_ref, gate_w_ref,
    mid_gain_ref, mid_bias_ref, out_w_ref,
    left_f, right_buf, right_f, pp_out, pp_in, gp_buf, gp_f, gl_f, gr_out, gr_in,
    load_sem,
    r_send, r_recv, pp_send, pp_recv, gp_send, gp_recv, gr_send, gr_recv,
    norm_buf, norm_sems,
    *sums_refs,
):
    block, _, width = pair_ref.shape
    half = out_w_ref.shape[0]
    cells = block * block
    row, col = lax.axis_index("row"), lax.axis_index("col")

    def remote(src, dst, send, recv, to_row, to_col):
        return pltpu.make_async_remote_copy(
            src_ref=src, dst_ref=dst, send_sem=send, recv_sem=recv,
            device_id={"row": to_row, "col": to_col}, device_id_type=MESH,
        )

    def wrap(place):
        return jnp.where(place >= n, place - n, place)

    def peers(body, first=1):
        def step(d, carry):
            body(d)
            return carry

        lax.fori_loop(first, n, step, 0, unroll=n <= 4)

    chip = col // 2
    core = col - 2 * chip

    def near_row(d):
        both = jnp.minimum(row, n - 1 - row)
        paired = row + (2 * (d % 2) - 1) * ((d + 1) // 2)
        alone = jnp.where(row < n - 1 - row, row + d - both, row - d + both)
        return jnp.where(d <= 2 * both, paired, alone)

    def near_col(d):
        along = chip + d // 2
        along = jnp.where(along >= n // 2, along - n // 2, along)
        swap = d % 2
        return along * 2 + core + swap - 2 * core * swap

    def arrived(buf, recv, slot):
        remote(buf.at[slot], buf.at[slot], recv.at[slot], recv.at[slot], row, col).wait_recv()

    loads = [
        pltpu.make_async_copy(src, dst, load_sem.at[at])
        for at, (src, dst) in enumerate(
            (
                (pair_hbm, pair_ref), (right_w_hbm, right_w_ref), (in_gain_hbm, in_gain_ref),
                (in_bias_hbm, in_bias_ref), (left_w_hbm, left_w_ref), (gate_w_hbm, gate_w_ref),
                (cot_hbm, cot_ref), (out_w_hbm, out_w_ref), (mid_gain_hbm, mid_gain_ref),
                (mid_bias_hbm, mid_bias_ref),
            )
        )
    ]
    for load in loads:
        load.start()
    barrier = pltpu.get_barrier_semaphore()

    everyone = n * n
    me = row * n + col

    def others(body):
        def one_row(d_row, first):
            to_row = wrap(row + d_row)

            def step(d_col, carry):
                to_col = wrap(col + d_col)
                body(to_row * n + to_col, to_row, to_col)
                return carry

            lax.fori_loop(first, n, step, 0, unroll=n <= 4)

        def step_row(d_row, carry):
            one_row(d_row, 0)
            return carry

        lax.fori_loop(1, n, step_row, 0, unroll=n <= 4)
        one_row(0, 1)

    def greet(other, to_row, to_col):
        pl.semaphore_signal(
            barrier, inc=1, device_id={"row": to_row, "col": to_col}, device_id_type=MESH
        )

    others(greet)

    cell = lax.broadcasted_iota(jnp.int32, (cells, 1), 0)
    count = lengths_ref[0]
    mask = jnp.where(
        (row * block + cell // block < count) & (col * block + cell % block < count), 1.0, 0.0
    ).astype(F32)
    for load in loads[:4]:
        load.wait()
    in_gain, in_bias = in_gain_ref[...], in_bias_ref[...]
    normed, scaled_in, spread_in = normalize(
        pair_ref[...].reshape(cells, width).astype(F32), in_gain, in_bias
    )
    normed_b = normed.astype(BF16)

    right_all = dot(normed_b, right_w_ref[...])
    right_values, right_switch = right_all[:, :half], jax.nn.sigmoid(right_all[:, half:])
    right_gate = mask * right_switch
    right_buf[row] = (right_gate * right_values).astype(BF16).reshape(block, block, half)
    pl.semaphore_wait(barrier, everyone - 1)

    def right_copy(d):
        return remote(
            right_buf.at[row], right_buf.at[row], r_send.at[d], r_recv.at[row], wrap(row + d), col
        )

    peers(lambda d: right_copy(d).start())

    for load in loads[4:]:
        load.wait()
    left_all = dot(normed_b, left_w_ref[...])
    left_values, left_switch = left_all[:, :half], jax.nn.sigmoid(left_all[:, half:])
    left_gate = mask * left_switch
    left_f[...] = (left_gate * left_values).astype(BF16).astype(F32).reshape(block, block, half)

    switch_out = jax.nn.sigmoid(dot(normed_b, gate_w_ref[...]))
    upstream = cot_ref[...].reshape(cells, width).astype(F32)
    grad_update = (upstream * switch_out).astype(BF16)
    grad_mixed = dot_t(grad_update, out_w_ref[...])

    def pp_copy(to_col):
        return remote(pp_out.at[to_col], pp_in.at[col], pp_send.at[to_col], pp_recv.at[col], row, to_col)

    def product_block(d, wait):
        at = near_row(d) if wait else row
        if wait:
            arrived(right_buf, r_recv, at)
        right_f[at] = right_buf[at].astype(F32)

        def one(i, carry):
            near = left_f[i]
            rows = [jnp.sum(near * right_f[at, j], axis=0, keepdims=True) for j in range(block)]
            pp_out[at, i] = jnp.concatenate(rows, axis=0).astype(BF16)
            return carry

        lax.fori_loop(0, block, one, 0)

        @pl.when(at != col)
        def _():
            pp_copy(at).start()

    product_block(0, False)
    peers(lambda d: product_block(d, True))

    def summed(own, buf, first):
        def step(d, total):
            slot = wrap(first + d)
            return total + buf[slot].astype(F32)

        return lax.fori_loop(1, n, step, own.astype(F32)).reshape(cells, half)

    peers(lambda d: arrived(pp_in, pp_recv, wrap(col + d)))
    product = summed(pp_out[col], pp_in, col)
    mid_gain = mid_gain_ref[...]
    mixed, scaled_mid, spread_mid = normalize(product, mid_gain, mid_bias_ref[...])
    grad_prod = norm_back(grad_mixed, mid_gain, scaled_mid, spread_mid)
    gp_buf[col] = grad_prod.astype(BF16).reshape(block, block, half)

    def gp_copy(d):
        return remote(
            gp_buf.at[col], gp_buf.at[col], gp_send.at[d], gp_recv.at[col], row, wrap(col + d)
        )

    peers(lambda d: gp_copy(d).start())

    def gr_copy(to_row):
        return remote(gr_out.at[to_row], gr_in.at[row], gr_send.at[to_row], gr_recv.at[row], to_row, col)

    def gr_block(d, wait):
        at = near_col(d) if wait else col
        if wait:
            arrived(gp_buf, gp_recv, at)
        gp_f[at] = gp_buf[at].astype(F32)

        def one(j, carry):
            total = gp_f[at, 0, pl.ds(j, 1), :] * left_f[0]
            for i in range(1, block):
                total = total + gp_f[at, i, pl.ds(j, 1), :] * left_f[i]
            gr_out[at, j] = total.astype(BF16)
            return carry

        lax.fori_loop(0, block, one, 0)

        @pl.when(at != row)
        def _():
            gr_copy(at).start()

    class Direct:
        def __init__(self, src, into, fin, sems):
            self.src, self.into, self.fin, self.sems = src, into, fin, sems

        def fill(self, parts):
            per = everyone // len(parts)
            for at, part in enumerate(parts):
                self.src[at * per : (at + 1) * per] = part.astype(BF16).reshape(
                    per, self.src.shape[1], part.shape[-1]
                )

        def start_1(self):
            others(
                lambda other, *to: remote(
                    self.src.at[other], self.into.at[me], self.sems.at[0], self.sems.at[1], *to
                ).start()
            )

        def all_but_one(self, send, recv):
            rest = self.into.at[0 : everyone - 1]
            return remote(rest, rest, self.sems.at[send], self.sems.at[recv], row, col)

        def start_2(self):
            self.into[me] = self.src[me]
            self.all_but_one(0, 1).wait_recv()
            self.fin[me] = jnp.sum(self.into[...].astype(F32), axis=0).astype(BF16)
            others(
                lambda other, *to: remote(
                    self.fin.at[me], self.fin.at[me], self.sems.at[2], self.sems.at[3], *to
                ).start()
            )

        def start_3(self):
            pass

        def finish(self, count):
            self.all_but_one(2, 3).wait_recv()
            per = everyone // count
            chunk, lanes = self.fin.shape[1:]
            return [
                self.fin[at * per : (at + 1) * per].astype(F32).reshape(per * chunk, lanes)
                for at in range(count)
            ]

        def drain(self):
            self.all_but_one(0, 1).wait_send()
            self.all_but_one(2, 3).wait_send()

    class Staged:
        def __init__(self, src, into, mid, fin, sems):
            self.src, self.into, self.mid, self.fin, self.sems = src, into, mid, fin, sems
            self.chunk = fin.shape[1]

        def fill(self, parts):
            per = n // len(parts)
            for at, part in enumerate(parts):
                self.src[at * per : (at + 1) * per] = part.astype(BF16).reshape(
                    per, self.chunk, part.shape[-1]
                )

        def copy_1(self, d):
            to_col = wrap(col + d)
            return remote(
                self.src.at[to_col], self.into.at[col], self.sems.at[0], self.sems.at[1], row, to_col
            )

        def copy_2(self, d):
            to_row = wrap(row + d)
            return remote(
                self.mid.at[row], self.mid.at[row], self.sems.at[2], self.sems.at[3], to_row, col
            )

        def copy_3(self, d):
            to_col = wrap(col + d)
            return remote(
                self.fin.at[col], self.fin.at[col], self.sems.at[4], self.sems.at[5], row, to_col
            )

        def all_but_one(self, send, recv):
            rest = self.fin.at[0 : n - 1]
            return remote(rest, rest, self.sems.at[send], self.sems.at[recv], row, col)

        def start_1(self):
            peers(lambda d: self.copy_1(d).start())

        def start_2(self):
            self.into[col] = self.src[col]
            self.all_but_one(0, 1).wait_recv()
            self.mid[row] = jnp.sum(self.into[...].astype(F32), axis=0).astype(BF16)
            peers(lambda d: self.copy_2(d).start())

        def start_3(self):
            self.all_but_one(2, 3).wait_recv()
            self.fin[col] = jnp.sum(self.mid[...].astype(F32), axis=0).astype(BF16)
            peers(lambda d: self.copy_3(d).start())

        def finish(self, count):
            self.all_but_one(4, 5).wait_recv()
            per = n // count
            return [
                self.fin[at * per : (at + 1) * per].astype(F32).reshape(per * self.chunk, self.fin.shape[-1])
                for at in range(count)
            ]

        def drain(self):
            for at in (0, 2, 4):
                self.all_but_one(at, at + 1).wait_send()

    sums_a, sums_b = Staged(*sums_refs[0:5]), Staged(*sums_refs[5:10])
    sums_c = (Direct if len(sums_refs) == 14 else Staged)(*sums_refs[10:])

    gr_block(0, False)

    mixed_b = mixed.astype(BF16)
    update = dot(mixed_b, out_w_ref[...])
    result_ref[...] = (switch_out * update).astype(BF16).reshape(block, block, width)
    grad_gate = (upstream * update * switch_out * (1.0 - switch_out)).astype(BF16)

    peers(lambda d: gr_block(d, True))
    sums_a.fill([cell_sum(normed_b, grad_gate), cell_sum(mixed_b, grad_update)])
    sums_a.start_1()

    def gl_row(i, carry):
        def step(at, total):
            for j in range(block):
                total = total + gp_f[at, i, j : j + 1, :] * right_f[at, j]
            return total

        gl_f[i] = lax.fori_loop(0, n, step, jnp.zeros((block, half), F32))
        return carry

    lax.fori_loop(0, block, gl_row, 0)

    def gated_back(total, gate, values, switch):
        first = total * gate
        return first.astype(BF16), (first * values * (1.0 - switch)).astype(BF16)

    left_1, left_2 = gated_back(gl_f[...].reshape(cells, half), left_gate, left_values, left_switch)

    sums_b.fill([cell_sum(normed_b, left_1), cell_sum(normed_b, left_2)])
    sums_b.start_1()
    left_w, right_w = left_w_ref[...], right_w_ref[...]
    grad_normed = dot_t(grad_gate, gate_w_ref[...])
    grad_normed = grad_normed + dot_t(left_1, left_w[:, :half]) + dot_t(left_2, left_w[:, half:])
    sums_a.start_2()

    peers(lambda d: arrived(gr_in, gr_recv, wrap(row + d)))
    grad_right = summed(gr_out[row], gr_in, row)
    right_1, right_2 = gated_back(grad_right, right_gate, right_values, right_switch)
    sums_c.fill([cell_sum(normed_b, right_1), cell_sum(normed_b, right_2)])
    sums_c.start_1()

    grad_normed = grad_normed + dot_t(right_1, right_w[:, :half]) + dot_t(right_2, right_w[:, half:])

    place = lax.broadcasted_iota(jnp.int32, (8, width), 0)
    own = jnp.zeros((8, width), F32)
    for at, term in enumerate((grad_normed * scaled_in, grad_normed, grad_mixed * scaled_mid, grad_mixed)):
        own = jnp.where(place == at, jnp.sum(term, axis=0, keepdims=True), own)
    norm_buf[me] = own
    others(
        lambda other, *to: remote(
            norm_buf.at[me], norm_buf.at[me], norm_sems.at[0], norm_sems.at[1], *to
        ).start()
    )
    sums_b.start_2()
    sums_a.start_3()
    sums_c.start_2()
    grad_pair_ref[...] = norm_back(grad_normed, in_gain, scaled_in, spread_in).reshape(block, block, width)
    sums_b.start_3()
    sums_c.start_3()

    factor = 1.0 / (block * n)
    parts = sums_a.finish(2)
    d_gate_ref[...] = parts[0] * factor
    d_out_ref[...] = parts[1] * factor
    parts = sums_b.finish(2)
    d_left_ref[:, :half] = parts[0] * factor
    d_left_ref[:, half:] = parts[1] * factor
    rest = norm_buf.at[0 : everyone - 1]
    rest_copy = remote(rest, rest, norm_sems.at[0], norm_sems.at[1], row, col)
    rest_copy.wait_recv()
    norms = jnp.sum(norm_buf[...], axis=0) * factor
    d_in_ref[...] = norms[0:2]
    d_mid_ref[...] = norms[2:4]
    rest_copy.wait_send()

    for copy in (right_copy, gp_copy):
        peers(lambda d, copy=copy: copy(d).wait_send())
    peers(lambda d: pp_copy(wrap(col + d)).wait_send())
    peers(lambda d: gr_copy(wrap(row + d)).wait_send())
    sums_a.drain()
    sums_b.drain()
    parts = sums_c.finish(2)
    d_right_ref[:, :half] = parts[0] * factor
    d_right_ref[:, half:] = parts[1] * factor
    sums_c.drain()


def write_out(*refs):
    sem = refs[-1]
    count = len(refs) // 2
    copies = [
        pltpu.make_async_copy(src, dst, sem.at[at])
        for at, (src, dst) in enumerate(zip(refs[:count], refs[count : 2 * count]))
    ]
    for copy in copies:
        copy.start()
    for copy in copies:
        copy.wait()


def solution(mesh):
    n = mesh.shape["row"]
    assert mesh.shape["col"] == n and n % 4 == 0

    def on_device(
        pair, cotangent, lengths, in_gain, in_bias, left_w, right_w, gate_w, mid_gain, mid_bias, out_w
    ):
        block, _, width = pair.shape
        half = left_w.shape[1] // 2
        vmem = pl.BlockSpec(memory_space=pltpu.VMEM)
        smem = pl.BlockSpec(memory_space=pltpu.SMEM)
        hbm = pl.BlockSpec(memory_space=pltpu.HBM)
        operands = [
            pair, cotangent, in_gain.reshape(1, -1), in_bias.reshape(1, -1), left_w, right_w, gate_w,
            mid_gain.reshape(1, -1), mid_bias.reshape(1, -1), out_w,
        ]

        def blocks(dtype, *lead):
            return pltpu.VMEM(lead + (block, block, half), dtype)

        def reduce_bufs(rows, direct=False):
            sems = pltpu.SemaphoreType.DMA((6,))
            share = rows // (n * n)
            if direct and share % ROWS == 0:
                return [pltpu.VMEM((n * n, share, half), BF16)] * 3 + [sems]
            return [pltpu.VMEM((n, rows // n, half), BF16)] * 4 + [sems]

        shape = jax.ShapeDtypeStruct
        out_shape = (
            shape(pair.shape, BF16),
            shape(pair.shape, F32),
            shape(left_w.shape, F32),
            shape(right_w.shape, F32),
            shape(gate_w.shape, F32),
            shape(out_w.shape, F32),
            shape((2, width), F32),
            shape((2, half), F32),
        )
        outs = pl.pallas_call(
            functools.partial(kernel, n),
            out_shape=out_shape,
            in_specs=[smem] + [hbm] * 10,
            out_specs=[vmem] * 8,
            scratch_shapes=[
                *[pltpu.VMEM(x.shape, x.dtype) for x in operands],
                blocks(F32), blocks(BF16, n), blocks(F32, n), blocks(BF16, n), blocks(BF16, n),
                blocks(BF16, n), blocks(F32, n), blocks(F32), blocks(BF16, n), blocks(BF16, n),
                pltpu.SemaphoreType.DMA((10,)),
                *[pltpu.SemaphoreType.DMA((n,))] * 8,
                pltpu.VMEM((n * n, 8, width), F32),
                pltpu.SemaphoreType.DMA((2,)),
                *reduce_bufs(gate_w.shape[0] + out_w.shape[0]),
                *reduce_bufs(2 * left_w.shape[0]),
                *reduce_bufs(2 * right_w.shape[0], direct=True),
            ],
            compiler_params=pltpu.CompilerParams(
                collective_id=0, has_side_effects=True, vmem_limit_bytes=63 * 1024 * 1024
            ),
        )(lengths, *operands)
        return pl.pallas_call(
            write_out,
            out_shape=out_shape,
            in_specs=[vmem] * 8,
            out_specs=[hbm] * 8,
            scratch_shapes=[pltpu.SemaphoreType.DMA((8,))],
        )(*outs)

    cells = P(("grp", "row"), "col", None)
    return jax.shard_map(
        on_device,
        mesh=mesh,
        in_specs=(cells, cells, P("grp")) + (P(),) * 8,
        out_specs=(cells, cells) + (P("grp", None),) * 6,
        check_vma=False,
    )
```

time: 45.4 us -> 44.8 us (0.987)
  Pallas kernels: 43.9 us -> 43.3 us
    pallas_call x1, Pallas kernels: 41.9 us -> 41.4 us  [on_device(): pl.pallas_call(functools.partial(kernel, n), out_shape=out_shape, in_spec...]
where the time goes in v3:
time: 44.8 us; the launch traced here: 44.6 us
  Pallas kernels  43.3 us (97%)
  between operations  1.29 us (3%)
    pallas_call x1, Pallas kernels, on_device(): pl.pallas_call(functools.partial(kernel, n), out_shape=out_shape, in_spec...  41.4 us
    pallas_call x1, Pallas kernels, on_device(): pl.pallas_call(write_out, out_shape=out_shape, in_specs=[vmem] * 8, out_s...  1.98 us

profile of v3, /device:TPU:0, one launch (start us, length us, event | category | flops | bytes accessed | tf_op | source)
XLA Modules:
  0.0 44.6 jit_solution(9236778553555127777)
XLA Ops:
  1.3 41.4 %shard_map.170 = (bf16[16,16,128]{2,1,0:T(8,128)(2,1)}, f32[16,16,128]{2,1,0:T(8,128)}, f32[128,256]{1,0:T(8,128)}, f32[128,256]{1,0:T(8,128)}, f32[128,128]{1,0...) custom-call(s32[1]{0:T(128)S(6)} %copy.19.lengths_ref, bf16[16,16,128]{2,1,0:T(8,128)(2,1)} %pair_hbm.1, ...), custom_call_target="tpu_custom_call" | custom-call | tf_op jit(solution)/shard_map/pallas_call | solution.py:491
  42.7 2.0 %shard_map.171 = (bf16[16,16,128]{2,1,0:T(8,128)(2,1)}, f32[16,16,128]{2,1,0:T(8,128)}, f32[128,256]{1,0:T(8,128)}, f32[128,256]{1,0:T(8,128)}, f32[128,128]{1,0...) custom-call(bf16[16,16,128]{2,1,0:T(8,128)(2,1)} %get-tuple-element.16.refs_0_, ...), custom_call_target="tpu_custom_call" | custom-call | tf_op jit(solution)/shard_map/pallas_call | solution.py:512
